TPU v7x, 32 devices: a whole 2x2x4 slice. The times are simulated.
32 devices in a mesh: group: 2 (over x), row: 16 (over z, y, core), feat: 1.
Axes of the slice: x: 2, y: 2, z: 4, core: 2. Of those that a mesh axis runs over, the one named last changes fastest.
Arguments:
- cells: bfloat16 [1024, 256, 128], P(('group', 'row'), 'feat'), parts along dimension 0, may hold values from -6 to 6
- is_context: int32 [1024], P(('group', 'row')), parts along dimension 0, may hold values from 0 to 1, as said below
- labels: int32 [1024], P(('group', 'row', 'feat')), parts along dimension 0, may hold values from 0 to 9
- inducing: bfloat16 [96, 128], replicated, may hold values from -6 to 6
- induce_query: bfloat16 [128, 128], replicated, may hold values from -1.5 to 1.5
- column_kvo: bfloat16 [3, 128, 128], replicated, may hold values from -0.5 to 0.5
- cell_qkvo: bfloat16 [4, 128, 128], replicated, may hold values from -0.5 to 0.5
- class_tokens: bfloat16 [4, 128], replicated, may hold values from -6 to 6
- class_query: bfloat16 [128, 128], replicated, may hold values from -1.5 to 1.5
- row_kvo: bfloat16 [3, 128, 128], replicated, may hold values from -0.5 to 0.5
- label_table: bfloat16 [10, 512], replicated, may hold values from -6 to 6
- icl_query: bfloat16 [512, 512], replicated, may hold values from -0.75 to 0.75
- icl_kvo: bfloat16 [3, 512, 512], replicated, may hold values from -0.25 to 0.25
Outputs:
- row_outputs: bfloat16 [1024, 512], P(('group', 'row', 'feat')), parts along dimension 0
There are 2 independent parts, one for each index of `group`. A program takes and returns all parts, laid end to end along the dimension named above; an argument that names none is the same for every part. Nothing has to cross between parts.
Inputs may be any that keep to these rules, and one draw needn't show every extreme that they name: `is_context`: 1 marks a labelled context row, 0 a query row; every window holds context rows.
All inputs are finite; a program needn't handle non-finite values.
Results may differ from a plain program's by a relative error of at most 0.017.
Values may be sent and summed in bfloat16 or wider, within the bound.
A program may use at most 128 MiB of HBM per device.

v0:
```python
import math

import jax
import jax.numpy as jnp
from jax import lax
from jax.experimental import pallas as pl
from jax.experimental.pallas import tpu as pltpu
from jax.sharding import PartitionSpec as P

HEADS = 4
ROW_HEADS = 8
EPSILON = 1e-06
LOG2E = math.log2(math.e)

F32 = jnp.float32
BF16 = jnp.bfloat16


def mm(a, b):
    return jnp.dot(a, b, preferred_element_type=F32)


def mm_nt(a, b):
    return lax.dot_general(a, b, (((1,), (1,)), ((), ())), preferred_element_type=F32)


def flip(w):
    return w.astype(F32).T.astype(BF16)


def head_rows(shape, row_block, lane_block, n):
    rows = lax.broadcasted_iota(jnp.int32, shape, 0) // row_block
    lanes = lax.broadcasted_iota(jnp.int32, shape, 1) // lane_block
    return lax.rem(rows, n) == lax.rem(lanes, n)


def row_queries(ct, class_query):
    n_class, width = ct.shape
    rq = mm(ct, class_query).astype(BF16).astype(F32)
    shape = (n_class * ROW_HEADS, width)
    rq = jnp.broadcast_to(rq[:, None, :], (n_class, ROW_HEADS, width)).reshape(shape)
    return jnp.where(head_rows(shape, 1, width // ROW_HEADS, ROW_HEADS), rq, 0.0)


def prepare(ind, iq_w, ckvo, cqkvo, ct, cq_w, rkvo, wcol, wrow, wt):
    n_ind, width = ind.shape
    iq = mm(ind[...], iq_w[...]).astype(BF16).astype(F32)
    iq = jnp.concatenate([iq] * HEADS, axis=0)
    iq = jnp.where(head_rows(iq.shape, n_ind, width // HEADS, HEADS), iq, 0.0).astype(BF16)
    scale = LOG2E / math.sqrt(width // HEADS)
    wcol[...] = (mm_nt(iq, ckvo[0]) * scale).astype(BF16)
    rq = row_queries(ct[...], cq_w[...]).astype(BF16)
    row_scale = LOG2E / math.sqrt(width // ROW_HEADS)
    wrow[...] = (mm_nt(rq, rkvo[0]) * row_scale).astype(BF16)
    wt[0] = flip(cqkvo[0])
    wt[1] = flip(cqkvo[2])
    wt[2] = flip(cqkvo[3])
    wt[3] = flip(rkvo[1])


def feature(x, maskb, ind, ckvo, cqkvo, wcol, wrow, wt):
    n_ind, width = ind.shape
    head = width // HEADS
    xt = x.T
    weight = jnp.exp2(mm(wcol[...], xt)).astype(BF16)
    values = mm(x, ckvo[1]).astype(BF16) * maskb
    numer = mm(weight, jnp.concatenate([values, maskb], axis=1))
    ratio = numer[:, :width] / numer[:, width:]
    lane_head = lax.broadcasted_iota(jnp.int32, (n_ind, width), 1) // head
    col_mix = ratio[:n_ind]
    for h in range(1, HEADS):
        col_mix = jnp.where(lane_head == h, ratio[h * n_ind : (h + 1) * n_ind], col_mix)
    summary = (ind[...].astype(F32) + mm(col_mix.astype(BF16), ckvo[2])).astype(BF16)
    scale = LOG2E / math.sqrt(head)
    keys = mm(summary, cqkvo[1]) * scale
    keys = jnp.concatenate([keys] * HEADS, axis=0)
    keys = jnp.where(head_rows(keys.shape, n_ind, head, HEADS), keys, 0.0).astype(BF16)
    sum_values = mm_nt(wt[1], jnp.concatenate([summary] * HEADS, axis=0))
    sum_values = jnp.where(head_rows(sum_values.shape, head, n_ind, HEADS), sum_values, 0.0)
    sum_values = sum_values.astype(BF16)
    query = mm(wt[0], xt).astype(BF16)
    cell = jnp.exp2(mm(keys, query))
    blocks = []
    for h in range(HEADS):
        part = cell[h * n_ind : (h + 1) * n_ind]
        blocks.append((part * (1.0 / jnp.sum(part, axis=0, keepdims=True))).astype(BF16))
    cell = jnp.concatenate(blocks, axis=0)
    mix = mm(sum_values, cell).astype(BF16)
    out = xt.astype(F32) + mm(wt[2], mix)
    inv = lax.rsqrt(jnp.mean(out * out, axis=0, keepdims=True) + EPSILON)
    embedded = (out * inv).astype(BF16)
    row_weight = jnp.exp2(mm(wrow[...], embedded))
    row_values = mm(wt[3], embedded).astype(BF16).astype(F32)
    return row_weight, row_values


def accumulate(terms, acc, den, n_class):
    width = terms[0][1].shape[0]
    total = terms[0][0]
    for weight, _ in terms[1:]:
        total = total + weight
    den[...] += total
    for c in range(n_class):
        add = None
        for weight, values in terms:
            w = weight[c * ROW_HEADS : (c + 1) * ROW_HEADS].astype(BF16).astype(F32)
            n = w.shape[1]
            w = jnp.broadcast_to(w[:, None, :], (ROW_HEADS, width // ROW_HEADS, n)).reshape(width, n)
            add = w * values if add is None else add + w * values
        acc[c] += add


def finish(acc, den, out_ref):
    n_class, width, _ = acc.shape
    for c in range(n_class):
        out_ref[:, c * width : (c + 1) * width] = acc[c].T.astype(BF16)
    d = den[...]
    pad = jnp.zeros((width - d.shape[0], d.shape[1]), F32)
    out_ref[:, n_class * width :] = jnp.concatenate([d, pad], axis=0).T.astype(BF16)


def column_kernel(x_ref, maskb, ind, iq_w, ckvo, cqkvo, ct, cq_w, rkvo, out_ref, wcol, wrow, wt, acc, den):
    step = pl.program_id(0)

    @pl.when(step == 0)
    def _():
        prepare(ind, iq_w, ckvo, cqkvo, ct, cq_w, rkvo, wcol, wrow, wt)
        acc[...] = jnp.zeros_like(acc)
        den[...] = jnp.zeros_like(den)

    n_src, n_feat, n_rows, width = x_ref.shape
    terms = []
    for f in range(n_feat):
        x = x_ref[:, f].reshape(n_src * n_rows, width)
        terms.append(feature(x, maskb[...], ind, ckvo, cqkvo, wcol, wrow, wt))
    accumulate(terms, acc, den, ct.shape[0])

    @pl.when(step == pl.num_programs(0) - 1)
    def _():
        finish(acc, den, out_ref)


def embed_rows(total, ct, cq_w, rkvo, context, labels, table):
    n_class, width = ct.shape
    n_rows = total.shape[0]
    queries = row_queries(ct[...], cq_w[...])
    keys = mm(ct[...], rkvo[0]).astype(BF16).astype(F32)
    values = mm(ct[...], rkvo[1]).astype(BF16).astype(F32)
    scale = LOG2E / math.sqrt(width // ROW_HEADS)
    cls_den = jnp.zeros((n_class * ROW_HEADS, 1), F32)
    cls_num = jnp.zeros((n_class * ROW_HEADS, width), F32)
    for t in range(n_class):
        w = jnp.exp2(jnp.sum(queries * keys[t : t + 1], axis=1, keepdims=True) * scale)
        cls_den = cls_den + w
        cls_num = cls_num + w.astype(BF16).astype(F32) * values[t : t + 1]
    shape = cls_num.shape
    own = head_rows(shape, 1, width // ROW_HEADS, ROW_HEADS)
    cls_num = jnp.where(own, cls_num, 0.0)
    cls_den = jnp.where(own, jnp.broadcast_to(cls_den, shape), 0.0)
    lane_head = lax.broadcasted_iota(jnp.int32, (n_rows, width), 1) // (width // ROW_HEADS)
    embeds = []
    for c in range(n_class):
        rows = slice(c * ROW_HEADS, (c + 1) * ROW_HEADS)
        numer = total[:, c * width : (c + 1) * width] + jnp.sum(cls_num[rows], axis=0, keepdims=True)
        denom = jnp.zeros((n_rows, width), F32)
        for h in range(ROW_HEADS):
            at = n_class * width + c * ROW_HEADS + h
            denom = jnp.where(lane_head == h, total[:, at : at + 1], denom)
        denom = denom + jnp.sum(cls_den[rows], axis=0, keepdims=True)
        mix = (numer / denom).astype(BF16)
        embeds.append((ct[c : c + 1].astype(F32) + mm(mix, rkvo[2])).astype(BF16))
    row_embed = jnp.concatenate(embeds, axis=1)
    label_vec = jnp.zeros((n_rows, n_class * width), F32)
    for k in range(table.shape[0]):
        label_vec = jnp.where(labels == k, table[k : k + 1].astype(F32), label_vec)
    icl_input = (row_embed.astype(F32) + context * label_vec).astype(BF16)
    return row_embed, icl_input


def embed_kernel(parts, ct, cq_w, rkvo, context, labels, table, embed_ref, input_ref):
    total = parts[0].astype(F32)
    for i in range(1, parts.shape[0]):
        total = total + parts[i].astype(F32)
    embed, icl = embed_rows(total, ct, cq_w, rkvo, context[...], labels[...], table)
    embed_ref[...] = embed
    input_ref[...] = icl


def in_context(embed, inputs, mask, icl_q, icl_kvo):
    width = embed.shape[1]
    head = width // HEADS
    query = mm(embed, icl_q[...]).astype(BF16)
    keys = mm(inputs, icl_kvo[0]).astype(BF16)
    values = mm(inputs, icl_kvo[1]).astype(BF16)
    scale = LOG2E / math.sqrt(head)
    mixes = []
    for h in range(HEADS):
        lanes = slice(h * head, (h + 1) * head)
        weight = jnp.exp2(mm_nt(query[:, lanes], keys[:, lanes]) * scale) * mask
        denom = jnp.sum(weight, axis=1, keepdims=True)
        mixes.append((mm(weight.astype(BF16), values[:, lanes]) / denom).astype(BF16))
    mix = jnp.concatenate(mixes, axis=1)
    return (embed.astype(F32) + mm(mix, icl_kvo[2])).astype(BF16)


def context_kernel(embed, inputs, mask, icl_q, icl_kvo, out_ref):
    out_ref[...] = in_context(embed[...], inputs[...], mask[...], icl_q, icl_kvo)


def whole(shape):
    return pl.BlockSpec(shape, lambda *_: (0,) * len(shape))


def on_device(
    cells,
    is_context,
    labels,
    inducing,
    induce_query,
    column_kvo,
    cell_qkvo,
    class_tokens,
    class_query,
    row_kvo,
    label_table,
    icl_query,
    icl_kvo,
):
    n_src = lax.axis_size("row")
    n_split = lax.axis_size("feat")
    n_rows, n_feat, width = cells.shape
    n_class = class_tokens.shape[0]
    all_rows = n_src * n_rows
    own_feat = n_feat // n_src
    out_rows = n_rows // n_split
    n_ind = inducing.shape[0]
    flags = (is_context == 1).astype(F32)
    window = lax.all_gather(flags, "row", axis=0, tiled=True)
    maskb = jnp.broadcast_to(window.astype(BF16)[:, None], (all_rows, width))

    by_feature = jnp.transpose(cells, (1, 0, 2)).reshape(n_src, own_feat, n_rows, width)
    x = lax.all_to_all(by_feature, "row", split_axis=0, concat_axis=0, tiled=True)
    per_step = 2 if own_feat % 2 == 0 else 1
    weights = (inducing, induce_query, column_kvo, cell_qkvo, class_tokens, class_query, row_kvo)
    sums = pl.pallas_call(
        column_kernel,
        grid=(own_feat // per_step,),
        in_specs=[
            pl.BlockSpec((n_src, per_step, n_rows, width), lambda i: (0, i, 0, 0)),
            whole((all_rows, width)),
        ]
        + [whole(w.shape) for w in weights],
        out_specs=whole((all_rows, (n_class + 1) * width)),
        out_shape=jax.ShapeDtypeStruct((all_rows, (n_class + 1) * width), BF16),
        scratch_shapes=[
            pltpu.VMEM((HEADS * n_ind, width), BF16),
            pltpu.VMEM((n_class * ROW_HEADS, width), BF16),
            pltpu.VMEM((4, width, width), BF16),
            pltpu.VMEM((n_class, width, all_rows), F32),
            pltpu.VMEM((n_class * ROW_HEADS, all_rows), F32),
        ],
        compiler_params=pltpu.CompilerParams(vmem_limit_bytes=48 * 2**20),
    )(x, maskb, *weights)

    n_parts = n_src * n_split
    parts = lax.all_to_all(
        sums.reshape(n_parts, out_rows, -1), ("row", "feat"), split_axis=0, concat_axis=0, tiled=True
    )
    own = lax.dynamic_slice_in_dim(flags, lax.axis_index("feat") * out_rows, out_rows)
    shape = jax.ShapeDtypeStruct((out_rows, n_class * width), BF16)
    row_embed, icl_input = pl.pallas_call(embed_kernel, out_shape=(shape, shape))(
        parts, class_tokens, class_query, row_kvo, own[:, None], labels[:, None], label_table
    )
    inputs = lax.all_gather(icl_input, ("row", "feat"), axis=0, tiled=True)
    return pl.pallas_call(
        context_kernel,
        out_shape=shape,
        compiler_params=pltpu.CompilerParams(vmem_limit_bytes=48 * 2**20),
    )(row_embed, inputs, window[None, :], icl_query, icl_kvo)


def solution(mesh):
    return jax.shard_map(
        on_device,
        mesh=mesh,
        in_specs=(
            P(("group", "row"), "feat", None),
            P(("group", "row")),
            P(("group", "row", "feat")),
            P(),
            P(),
            P(),
            P(),
            P(),
            P(),
            P(),
            P(),
            P(),
            P(),
        ),
        out_specs=P(("group", "row", "feat"), None),
        check_vma=False,
    )
```

profile of v0, /device:TPU:0, one launch (start us, length us, event | category | flops | bytes accessed | tf_op | source)
XLA Modules:
  0.0 156.9 jit_solution(2135068602535563056)
XLA Ops:
  0.0 4.3 %copy.14 = bf16[256,32,128]{2,1,0:T(8,128)(2,1)} copy(bf16[256,32,128]{2,0,1:T(8,128)(2,1)} %bitcast.10) | data formatting | bytes 4194304 | tf_op jit(solution)/shard_map/transpose | solution.py:241
  4.3 0.0 copy-start.4
  4.3 0.0 copy-start.5
  4.3 0.0 copy-start.6
  4.3 0.0 copy-start.8
  4.3 0.0 copy-start.9
  4.3 7.5 %all-to-all-start = ((bf16[16,16,32,128]{3,2,1,0:T(8,128)(2,1)}), bf16[16,16,32,128]{3,2,1,0:T(8,128)(2,1)S(1)}, u32[]{:S(2)}, u32[]{:S(2)}) async-start(bf16[16,16,32,128]{3,2,1,0:T(8,128)(2,1)} %bitcast.9), calls=%async_computation | async-start | bytes 4194304 | tf_op jit(solution)/shard_map/all_to_all | solution.py:242
  11.9 0.0 copy-done.13
  11.9 0.6 dynamic-slice
  13.1 0.0 copy-done.12
  13.2 0.1 fusion.1
  13.3 61.0 %all-reduce = f32[512]{0:T(512)S(1)} all-reduce(f32[512]{0:T(512)S(1)} %fusion.1), channel_id=1, replica_groups=mesh['group'=2,'row'=16,'feat'=1] {'row'}, use_global_device_ids=true, to_apply=%add | all-reduce | flops 512 | bytes 4096
  74.3 0.0 all-to-all-done.x_ref
  74.3 0.1 broadcast_in_dim.15.maskb
  74.4 0.0 copy-done.2
  74.4 0.0 copy-done.3
  74.4 0.0 copy-done.4
  74.4 0.0 copy-done.5
  74.4 0.0 copy-done.6
  74.4 0.0 copy-done.8
  74.5 0.0 copy-done.9
  74.5 0.0 copy-start.11
  74.5 29.9 %shard_map.127 = bf16[512,640]{1,0:T(8,128)(2,1)} custom-call(bf16[16,16,32,128]{3,2,1,0:T(8,128)(2,1)S(1)} %all-to-all-done.x_ref, bf16[512,128]{1,0:T(8,128)(2,1)S(1)} %broadcast_in_dim.15.maskb, bf16[96,128]{1,0:T(8,128)(2,1)S(1)} %copy-done.8, bf16[128,128]{1,0:T(8,128)(2,1)S(1)} %copy-done.6, bf16[3,128,128]{2,1,0:T(8,128)(2,1)S(1)} %copy-done.5, ...), custom_call_target="tpu_custom_call" | custom-call | tf_op jit(solution)/shard_map/pallas_call | solution.py:245
  104.4 7.7 %all-to-all-start.1 = ((bf16[16,32,640]{2,1,0:T(8,128)(2,1)}), bf16[16,32,640]{2,1,0:T(8,128)(2,1)S(1)}, u32[]{:S(2)}, u32[]{:S(2)}) async-start(bf16[16,32,640]{2,1,0:T(8,128)(2,1)} %bitcast.3), calls=%async_computation.1 | async-start | bytes 1310720 | tf_op jit(solution)/shard_map/all_to_all | solution.py:266
  112.1 0.7 copy.15.context
  112.8 0.7 copy.16.labels
  113.5 15.2 %all-to-all-done.1.parts = bf16[16,32,640]{2,1,0:T(8,128)(2,1)S(1)} async-done(((bf16[16,32,640]{2,1,0:T(8,128)(2,1)}), bf16[16,32,640]{2,1,0:T(8,128)(2,1)S(1)}, u32[]{:S(2)}, u32[]{:S(2)}) %all-to-all-start.1) | async-done | bytes 655392 | tf_op jit(solution)/shard_map/all_to_all | solution.py:266
  128.7 0.8 copy-done.10
  129.5 2.3 %shard_map.128 = (bf16[32,512]{1,0:T(8,128)(2,1)}, bf16[32,512]{1,0:T(8,128)(2,1)}) custom-call(bf16[16,32,640]{2,1,0:T(8,128)(2,1)} %copy-done.10, bf16[4,128]{1,0:T(4,128)(2,1)} %ct.3, bf16[128,128]{1,0:T(8,128)(2,1)} %cq_w.3, bf16[3,128,128]{2,1,0:T(8,128)(2,1)} %rkvo.3, f32[32,1]{1,0:T(8,128)} %copy.15.context, s32[32,1]{1,0:T(8,128)} %copy.16.labels, ...), custom_call_target="tpu_custom_call" | custom-call | tf_op jit(solution)/shard_map/pallas_call | solution.py:271
  131.8 22.1 %all_gather.7.inputs = bf16[512,512]{1,0:T(8,128)(2,1)S(1)} all-gather(bf16[32,512]{1,0:T(8,128)(2,1)} %get-tuple-element.8), channel_id=1, replica_groups=mesh['group'=2,'row'=16,'feat'=1] {'row','feat'}, dimensions={0}, use_global_device_ids=true | all-gather | bytes 557056 | tf_op jit(solution)/shard_map/all_gather | solution.py:274
  153.9 0.8 copy-done.7
  154.7 2.2 %shard_map.129 = bf16[32,512]{1,0:T(8,128)(2,1)} custom-call(bf16[32,512]{1,0:T(8,128)(2,1)S(1)} %copy-done.7, bf16[512,512]{1,0:T(8,128)(2,1)S(1)} %all_gather.7.inputs, f32[1,512]{1,0:T(1,128)S(1)} %bitcast.8, bf16[512,512]{1,0:T(8,128)(2,1)S(1)} %copy-done.1, bf16[3,512,512]{2,1,0:T(8,128)(2,1)S(1)} %copy-done), custom_call_target="tpu_custom_call" | custom-call | tf_op jit(solution)/shard_map/pallas_call | solution.py:275
  (14 shorter events, 0.0 us)
Async XLA Ops:
  4.3 7.6 %copy-start.13 = (u32[32]{0:T(128)S(1)}, u32[32]{0:T(128)}, u32[]{:S(2)}) copy-start(u32[32]{0:T(128)} %constant.8) | copy-start | bytes 388
  4.3 8.9 %copy-start.12 = (s32[32]{0:T(128)S(1)}, s32[32]{0:T(128)}, u32[]{:S(2)}) copy-start(s32[32]{0:T(128)} %param.14) | copy-start | bytes 388
  4.3 70.1 %copy-start.2 = (bf16[3,128,128]{2,1,0:T(8,128)(2,1)S(1)}, bf16[3,128,128]{2,1,0:T(8,128)(2,1)}, u32[]{:S(2)}) copy-start(bf16[3,128,128]{2,1,0:T(8,128)(2,1)} %rkvo.3) | copy-start | bytes 294916
  4.3 70.1 %copy-start.3 = (bf16[128,128]{1,0:T(8,128)(2,1)S(1)}, bf16[128,128]{1,0:T(8,128)(2,1)}, u32[]{:S(2)}) copy-start(bf16[128,128]{1,0:T(8,128)(2,1)} %cq_w.3) | copy-start | bytes 98308
  4.3 70.1 %copy-start.4 = (bf16[4,128,128]{2,1,0:T(8,128)(2,1)S(1)}, bf16[4,128,128]{2,1,0:T(8,128)(2,1)}, u32[]{:S(2)}) copy-start(bf16[4,128,128]{2,1,0:T(8,128)(2,1)} %cqkvo.1) | copy-start | bytes 393220
  4.3 70.1 %copy-start.5 = (bf16[3,128,128]{2,1,0:T(8,128)(2,1)S(1)}, bf16[3,128,128]{2,1,0:T(8,128)(2,1)}, u32[]{:S(2)}) copy-start(bf16[3,128,128]{2,1,0:T(8,128)(2,1)} %ckvo.1) | copy-start | bytes 294916
  4.3 70.1 %copy-start.6 = (bf16[128,128]{1,0:T(8,128)(2,1)S(1)}, bf16[128,128]{1,0:T(8,128)(2,1)}, u32[]{:S(2)}) copy-start(bf16[128,128]{1,0:T(8,128)(2,1)} %iq_w.1) | copy-start | bytes 98308
  4.3 70.1 %copy-start.8 = (bf16[96,128]{1,0:T(8,128)(2,1)S(1)}, bf16[96,128]{1,0:T(8,128)(2,1)}, u32[]{:S(2)}) copy-start(bf16[96,128]{1,0:T(8,128)(2,1)} %ind.1) | copy-start | bytes 73732
  4.3 70.1 %copy-start.9 = (bf16[4,128]{1,0:T(4,128)(2,1)S(1)}, bf16[4,128]{1,0:T(4,128)(2,1)}, u32[]{:S(2)}) copy-start(bf16[4,128]{1,0:T(4,128)(2,1)} %ct.3) | copy-start | bytes 3076
  4.3 69.9 %all-to-all-start = ((bf16[16,16,32,128]{3,2,1,0:T(8,128)(2,1)}), bf16[16,16,32,128]{3,2,1,0:T(8,128)(2,1)S(1)}, u32[]{:S(2)}, u32[]{:S(2)}) async-start(bf16[16,16,32,128]{3,2,1,0:T(8,128)(2,1)} %bitcast.9), calls=%async_computation | async-start | bytes 4194304 | tf_op jit(solution)/shard_map/all_to_all | solution.py:242
  74.5 38.3 %copy-start.11 = (s32[32]{0:T(128)S(1)}, s32[32]{0:T(128)}, u32[]{:S(2)}) copy-start(s32[32]{0:T(128)} %param.15) | copy-start | bytes 388
  104.4 49.6 %copy-start = (bf16[3,512,512]{2,1,0:T(8,128)(2,1)S(1)}, bf16[3,512,512]{2,1,0:T(8,128)(2,1)}, u32[]{:S(2)}) copy-start(bf16[3,512,512]{2,1,0:T(8,128)(2,1)} %icl_kvo.1) | copy-start | bytes 4718596
  104.4 49.6 %copy-start.1 = (bf16[512,512]{1,0:T(8,128)(2,1)S(1)}, bf16[512,512]{1,0:T(8,128)(2,1)}, u32[]{:S(2)}) copy-start(bf16[512,512]{1,0:T(8,128)(2,1)} %icl_q.1) | copy-start | bytes 1572868
  104.4 24.3 %all-to-all-start.1 = ((bf16[16,32,640]{2,1,0:T(8,128)(2,1)}), bf16[16,32,640]{2,1,0:T(8,128)(2,1)S(1)}, u32[]{:S(2)}, u32[]{:S(2)}) async-start(bf16[16,32,640]{2,1,0:T(8,128)(2,1)} %bitcast.3), calls=%async_computation.1 | async-start | bytes 1310720 | tf_op jit(solution)/shard_map/all_to_all | solution.py:266
  128.7 0.8 copy-start.10
  153.9 0.8 copy-start.7
where the time goes:
time: 157 us
  blocking collectives  83.1 us (53%)
  Pallas kernels  34.3 us (22%)
  starting transfers between devices  15.2 us (10%)
  waiting for transfers between devices  15.2 us (10%)
  local copies, waits for them, and re-layouts  8.03 us (5%)
    unnamed x1, blocking collectives  61 us
    pallas_call x1, Pallas kernels, on_device(): pl.pallas_call(column_kernel, grid=(own_feat // per_step,), in_specs=[pl....  29.9 us
    all_gather x1, blocking collectives, on_device(): inputs = lax.all_gather(icl_input, ('row', 'feat'), axis=0, tiled=True)  22.1 us
    all_to_all x1, waiting for transfers between devices, on_device(): lax.all_to_all(sums.reshape(n_parts, out_rows, -1), ('row', 'feat'), spli...  15.2 us
    all_to_all x1, starting transfers between devices, on_device(): lax.all_to_all(sums.reshape(n_parts, out_rows, -1), ('row', 'feat'), spli...  7.7 us
    all_to_all x1, starting transfers between devices, on_device(): lax.all_to_all(by_feature, 'row', split_axis=0, concat_axis=0, tiled=True)  7.53 us
    transpose x1, local copies, waits for them, and re-layouts, on_device(): jnp.transpose(cells, (1, 0, 2)).reshape(n_src, own_feat, n_rows, width)  4.27 us
  transfers between devices with their start and end apart: 2, of which 1 were waited for; matrix products, arithmetic and copies ran while one was open for 1% of the time, Pallas kernels for 0%

commit v1 on v0

--- a/solution.py
+++ b/solution.py
@@ -1,3 +1,4 @@
+import functools
 import math
 
 import jax
@@ -111,33 +112,15 @@
 
 
 def finish(acc, den, out_ref):
-    n_class, width, _ = acc.shape
+    n_class, width, n_rows = acc.shape
+    n_parts, out_rows, _ = out_ref.shape
     for c in range(n_class):
-        out_ref[:, c * width : (c + 1) * width] = acc[c].T.astype(BF16)
+        numer = acc[c].T.astype(BF16).reshape(n_parts, out_rows, width)
+        out_ref[:, :, c * width : (c + 1) * width] = numer
     d = den[...]
-    pad = jnp.zeros((width - d.shape[0], d.shape[1]), F32)
-    out_ref[:, n_class * width :] = jnp.concatenate([d, pad], axis=0).T.astype(BF16)
-
-
-def column_kernel(x_ref, maskb, ind, iq_w, ckvo, cqkvo, ct, cq_w, rkvo, out_ref, wcol, wrow, wt, acc, den):
-    step = pl.program_id(0)
-
-    @pl.when(step == 0)
-    def _():
-        prepare(ind, iq_w, ckvo, cqkvo, ct, cq_w, rkvo, wcol, wrow, wt)
-        acc[...] = jnp.zeros_like(acc)
-        den[...] = jnp.zeros_like(den)
-
-    n_src, n_feat, n_rows, width = x_ref.shape
-    terms = []
-    for f in range(n_feat):
-        x = x_ref[:, f].reshape(n_src * n_rows, width)
-        terms.append(feature(x, maskb[...], ind, ckvo, cqkvo, wcol, wrow, wt))
-    accumulate(terms, acc, den, ct.shape[0])
-
-    @pl.when(step == pl.num_programs(0) - 1)
-    def _():
-        finish(acc, den, out_ref)
+    pad = jnp.zeros((width - d.shape[0], n_rows), F32)
+    d = jnp.concatenate([d, pad], axis=0).T.astype(BF16)
+    out_ref[:, :, n_class * width :] = d.reshape(n_parts, out_rows, width)
 
 
 def embed_rows(total, ct, cq_w, rkvo, context, labels, table):
@@ -177,15 +160,6 @@
     return row_embed, icl_input
 
 
-def embed_kernel(parts, ct, cq_w, rkvo, context, labels, table, embed_ref, input_ref):
-    total = parts[0].astype(F32)
-    for i in range(1, parts.shape[0]):
-        total = total + parts[i].astype(F32)
-    embed, icl = embed_rows(total, ct, cq_w, rkvo, context[...], labels[...], table)
-    embed_ref[...] = embed
-    input_ref[...] = icl
-
-
 def in_context(embed, inputs, mask, icl_q, icl_kvo):
     width = embed.shape[1]
     head = width // HEADS
@@ -203,12 +177,128 @@
     return (embed.astype(F32) + mm(mix, icl_kvo[2])).astype(BF16)
 
 
-def context_kernel(embed, inputs, mask, icl_q, icl_kvo, out_ref):
-    out_ref[...] = in_context(embed[...], inputs[...], mask[...], icl_q, icl_kvo)
-
-
-def whole(shape):
-    return pl.BlockSpec(shape, lambda *_: (0,) * len(shape))
+MESH = pl.DeviceIdType.MESH
+
+
+def wait_bytes(ref, sem):
+    pltpu.make_async_copy(ref, ref, sem).wait()
+
+
+def window_kernel(
+    n_src, n_split, src, mask_src, context, labels, ind, iq_w, ckvo, cqkvo, ct, cq_w, rkvo, table, icl_q, icl_kvo,
+    out_ref, xbuf, mbuf, sums, pbuf, own_in, gbuf, wcol, wrow, wt, acc, den,
+    x_send, x_recv, x_local, m_send, m_recv, p_send, p_recv, g_send, g_recv, local,
+):
+    n_chunk, _, per, n_rows, width = xbuf.shape
+    n_class = ct.shape[0]
+    n_parts, out_rows, _ = pbuf.shape
+    all_rows = n_src * n_rows
+    me = lax.axis_index("row")
+    part = me * n_split + lax.axis_index("feat")
+
+    barrier = pltpu.get_barrier_semaphore()
+
+    def greet(d, carry):
+        peer = lax.rem(part + d, n_parts)
+        pl.semaphore_signal(
+            barrier, inc=1, device_id={"row": peer // n_split, "feat": lax.rem(peer, n_split)}, device_id_type=MESH
+        )
+        return carry
+
+    lax.fori_loop(1, n_parts, greet, 0)
+    pl.semaphore_wait(barrier, n_parts - 1)
+
+    def send_mask(d, carry):
+        peer = lax.rem(me + d, n_src)
+        pltpu.make_async_remote_copy(
+            src_ref=mask_src, dst_ref=mbuf.at[me], send_sem=m_send, recv_sem=m_recv,
+            device_id={"row": peer}, device_id_type=MESH,
+        ).start()
+        return carry
+
+    lax.fori_loop(1, n_src, send_mask, 0)
+
+    def send_chunk(k, carry):
+        def send(d, inner):
+            peer = lax.rem(me + d, n_src)
+            pltpu.make_async_remote_copy(
+                src_ref=src.at[peer, k], dst_ref=xbuf.at[k, me], send_sem=x_send.at[k], recv_sem=x_recv.at[k],
+                device_id={"row": peer}, device_id_type=MESH,
+            ).start()
+            return inner
+
+        lax.fori_loop(1, n_src, send, 0)
+        pltpu.make_async_copy(src.at[me, k], xbuf.at[k, me], x_local.at[k]).start()
+        return carry
+
+    lax.fori_loop(0, n_chunk, send_chunk, 0)
+    own_mask = pltpu.make_async_copy(mask_src, mbuf.at[me], local.at[0])
+    own_mask.start()
+
+    prepare(ind, iq_w, ckvo, cqkvo, ct, cq_w, rkvo, wcol, wrow, wt)
+    acc[...] = jnp.zeros_like(acc)
+    den[...] = jnp.zeros_like(den)
+    wait_bytes(mbuf.at[pl.ds(0, n_src - 1)], m_recv)
+    own_mask.wait()
+
+    def work(k, carry):
+        wait_bytes(xbuf.at[k, pl.ds(0, n_src - 1)], x_recv.at[k])
+        pltpu.make_async_copy(src.at[me, k], xbuf.at[k, me], x_local.at[k]).wait()
+        maskb = mbuf[...].reshape(all_rows, width)
+        terms = []
+        for f in range(per):
+            x = xbuf[k, :, f].reshape(all_rows, width)
+            terms.append(feature(x, maskb, ind, ckvo, cqkvo, wcol, wrow, wt))
+        accumulate(terms, acc, den, n_class)
+        return carry
+
+    lax.fori_loop(0, n_chunk, work, 0)
+    finish(acc, den, sums)
+
+    def exchange(make):
+        def send(d, carry):
+            peer = lax.rem(part + d, n_parts)
+            make(peer, {"row": peer // n_split, "feat": lax.rem(peer, n_split)}).start()
+            return carry
+
+        lax.fori_loop(1, n_parts, send, 0)
+
+    exchange(
+        lambda peer, device: pltpu.make_async_remote_copy(
+            src_ref=sums.at[peer], dst_ref=pbuf.at[part], send_sem=p_send, recv_sem=p_recv,
+            device_id=device, device_id_type=MESH,
+        )
+    )
+    own_sums = pltpu.make_async_copy(sums.at[part], pbuf.at[part], local.at[1])
+    own_sums.start()
+    mask = jnp.transpose(mbuf[...].reshape(all_rows, width).astype(F32))[:1]
+    own_sums.wait()
+    wait_bytes(pbuf.at[pl.ds(0, n_parts - 1)], p_recv)
+    total = jnp.sum(pbuf[...].astype(F32), axis=0)
+    embed, inputs = embed_rows(total, ct, cq_w, rkvo, context[...], labels[...], table)
+    own_in[...] = inputs
+    exchange(
+        lambda peer, device: pltpu.make_async_remote_copy(
+            src_ref=own_in, dst_ref=gbuf.at[part], send_sem=g_send, recv_sem=g_recv,
+            device_id=device, device_id_type=MESH,
+        )
+    )
+    own_inputs = pltpu.make_async_copy(own_in, gbuf.at[part], local.at[2])
+    own_inputs.start()
+    own_inputs.wait()
+    wait_bytes(gbuf.at[pl.ds(0, n_parts - 1)], g_recv)
+    window = gbuf[...].reshape(all_rows, n_class * width)
+    out_ref[...] = in_context(embed, window, mask, icl_q, icl_kvo)
+
+    wait_bytes(mbuf.at[pl.ds(0, n_src - 1)], m_send)
+
+    def sent(k, carry):
+        wait_bytes(xbuf.at[k, pl.ds(0, n_src - 1)], x_send.at[k])
+        return carry
+
+    lax.fori_loop(0, n_chunk, sent, 0)
+    wait_bytes(pbuf.at[pl.ds(0, n_parts - 1)], p_send)
+    wait_bytes(gbuf.at[pl.ds(0, n_parts - 1)], g_send)
 
 
 def on_device(
@@ -234,49 +324,63 @@
     own_feat = n_feat // n_src
     out_rows = n_rows // n_split
     n_ind = inducing.shape[0]
+    n_parts = n_src * n_split
+    per_chunk = 2 if own_feat % 2 == 0 else 1
+    n_chunk = own_feat // per_chunk
+    d3 = n_class * width
     flags = (is_context == 1).astype(F32)
-    window = lax.all_gather(flags, "row", axis=0, tiled=True)
-    maskb = jnp.broadcast_to(window.astype(BF16)[:, None], (all_rows, width))
-
-    by_feature = jnp.transpose(cells, (1, 0, 2)).reshape(n_src, own_feat, n_rows, width)
-    x = lax.all_to_all(by_feature, "row", split_axis=0, concat_axis=0, tiled=True)
-    per_step = 2 if own_feat % 2 == 0 else 1
-    weights = (inducing, induce_query, column_kvo, cell_qkvo, class_tokens, class_query, row_kvo)
-    sums = pl.pallas_call(
-        column_kernel,
-        grid=(own_feat // per_step,),
-        in_specs=[
-            pl.BlockSpec((n_src, per_step, n_rows, width), lambda i: (0, i, 0, 0)),
-            whole((all_rows, width)),
-        ]
-        + [whole(w.shape) for w in weights],
-        out_specs=whole((all_rows, (n_class + 1) * width)),
-        out_shape=jax.ShapeDtypeStruct((all_rows, (n_class + 1) * width), BF16),
+    mask = jnp.broadcast_to(flags.astype(BF16)[:, None], (n_rows, width))
+    by_feature = jnp.transpose(cells, (1, 0, 2)).reshape(n_src, n_chunk, per_chunk, n_rows, width)
+    own = lax.dynamic_slice_in_dim(flags, lax.axis_index("feat") * out_rows, out_rows)
+    vmem = pl.BlockSpec(memory_space=pltpu.VMEM)
+    dma = pltpu.SemaphoreType.DMA
+    return pl.pallas_call(
+        functools.partial(window_kernel, n_src, n_split),
+        in_specs=[pl.BlockSpec(memory_space=pl.ANY)] + [vmem] * 13,
+        out_specs=vmem,
+        out_shape=jax.ShapeDtypeStruct((out_rows, d3), BF16),
         scratch_shapes=[
+            pltpu.VMEM((n_chunk, n_src, per_chunk, n_rows, width), BF16),
+            pltpu.VMEM((n_src, n_rows, width), BF16),
+            pltpu.VMEM((n_parts, out_rows, d3 + width), BF16),
+            pltpu.VMEM((n_parts, out_rows, d3 + width), BF16),
+            pltpu.VMEM((out_rows, d3), BF16),
+            pltpu.VMEM((n_parts, out_rows, d3), BF16),
             pltpu.VMEM((HEADS * n_ind, width), BF16),
             pltpu.VMEM((n_class * ROW_HEADS, width), BF16),
             pltpu.VMEM((4, width, width), BF16),
             pltpu.VMEM((n_class, width, all_rows), F32),
             pltpu.VMEM((n_class * ROW_HEADS, all_rows), F32),
+            dma((n_chunk,)),
+            dma((n_chunk,)),
+            dma((n_chunk,)),
+            dma,
+            dma,
+            dma,
+            dma,
+            dma,
+            dma,
+            dma((3,)),
         ],
-        compiler_params=pltpu.CompilerParams(vmem_limit_bytes=48 * 2**20),
-    )(x, maskb, *weights)
-
-    n_parts = n_src * n_split
-    parts = lax.all_to_all(
-        sums.reshape(n_parts, out_rows, -1), ("row", "feat"), split_axis=0, concat_axis=0, tiled=True
+        compiler_params=pltpu.CompilerParams(
+            vmem_limit_bytes=48 * 2**20, collective_id=0, has_side_effects=True
+        ),
+    )(
+        by_feature,
+        mask,
+        own[:, None],
+        labels[:, None],
+        inducing,
+        induce_query,
+        column_kvo,
+        cell_qkvo,
+        class_tokens,
+        class_query,
+        row_kvo,
+        label_table,
+        icl_query,
+        icl_kvo,
     )
-    own = lax.dynamic_slice_in_dim(flags, lax.axis_index("feat") * out_rows, out_rows)
-    shape = jax.ShapeDtypeStruct((out_rows, n_class * width), BF16)
-    row_embed, icl_input = pl.pallas_call(embed_kernel, out_shape=(shape, shape))(
-        parts, class_tokens, class_query, row_kvo, own[:, None], labels[:, None], label_table
-    )
-    inputs = lax.all_gather(icl_input, ("row", "feat"), axis=0, tiled=True)
-    return pl.pallas_call(
-        context_kernel,
-        out_shape=shape,
-        compiler_params=pltpu.CompilerParams(vmem_limit_bytes=48 * 2**20),
-    )(row_embed, inputs, window[None, :], icl_query, icl_kvo)
 
 
 def solution(mesh):

time: 157 us -> 94.6 us (0.60)
  the two profiles are of different devices: /device:TPU:0 before, /device:TPU:29 now
where the time goes in v1:
time: 94.6 us; the launch traced here: 94.4 us
  Pallas kernels  88.9 us (94%)
  local copies, waits for them, and re-layouts  4.67 us (5%)
    pallas_call x1, Pallas kernels, on_device(): pl.pallas_call(functools.partial(window_kernel, n_src, n_split), in_specs...  88.9 us
    transpose x1, local copies, waits for them, and re-layouts, on_device(): jnp.transpose(cells, (1, 0, 2))  3.1 us

profile of v1, /device:TPU:29, one launch (start us, length us, event | category | flops | bytes accessed | tf_op | source)
XLA Modules:
  0.0 94.4 jit_solution(12899437802457505611)
XLA Ops:
  0.0 0.7 fusion
  0.7 0.1 broadcast_in_dim.12.mask_src
  0.7 0.1 copy.15.context
  0.8 0.7 copy.16.labels
  1.6 0.0 copy-start
  1.6 0.0 copy-start.1
  1.6 0.0 copy-start.2
  1.6 0.0 copy-start.3
  1.6 0.0 copy-start.4
  1.6 0.0 copy-start.5
  1.6 0.0 copy-start.6
  1.6 0.0 copy-start.7
  1.6 0.0 copy-start.8
  1.6 0.0 copy-start.9
  1.7 3.1 %copy.14 = bf16[256,32,128]{2,1,0:T(8,128)(2,1)S(1)} copy(bf16[256,32,128]{2,0,1:T(8,128)(2,1)} %bitcast.6) | data formatting | bytes 4194304 | tf_op jit(solution)/shard_map/transpose | solution.py:333
  4.8 0.0 copy-done
  4.8 0.0 copy-done.1
  4.8 0.0 copy-done.2
  4.8 0.0 copy-done.3
  4.8 0.0 copy-done.4
  4.8 0.0 copy-done.5
  4.8 0.0 copy-done.6
  4.8 0.0 copy-done.7
  4.8 0.0 copy-done.8
  4.8 0.0 copy-done.9
  4.9 88.9 %shard_map.127 = bf16[32,512]{1,0:T(8,128)(2,1)S(1)} custom-call(bf16[16,8,2,32,128]{4,3,2,1,0:T(8,128)(2,1)S(1)} %bitcast.5, bf16[32,128]{1,0:T(8,128)(2,1)S(1)} %broadcast_in_dim.12.mask_src, f32[32,1]{1,0:T(8,128)S(1)} %copy.15.context, s32[32,1]{1,0:T(8,128)S(1)} %copy.16.labels, bf16[96,128]{1,0:T(8,128)(2,1)S(1)} %copy-done.7, ...), custom_call_target="tpu_custom_call" | custom-call | tf_op jit(solution)/shard_map/pallas_call | solution.py:337
  93.8 0.6 copy.18
Async XLA Ops:
  1.6 3.2 %copy-start = (bf16[3,512,512]{2,1,0:T(8,128)(2,1)S(1)}, bf16[3,512,512]{2,1,0:T(8,128)(2,1)}, u32[]{:S(2)}) copy-start(bf16[3,512,512]{2,1,0:T(8,128)(2,1)} %icl_kvo.1) | copy-start | bytes 4718596
  1.6 3.2 %copy-start.1 = (bf16[512,512]{1,0:T(8,128)(2,1)S(1)}, bf16[512,512]{1,0:T(8,128)(2,1)}, u32[]{:S(2)}) copy-start(bf16[512,512]{1,0:T(8,128)(2,1)} %icl_q.1) | copy-start | bytes 1572868
  1.6 3.2 %copy-start.2 = (bf16[4,128,128]{2,1,0:T(8,128)(2,1)S(1)}, bf16[4,128,128]{2,1,0:T(8,128)(2,1)}, u32[]{:S(2)}) copy-start(bf16[4,128,128]{2,1,0:T(8,128)(2,1)} %cqkvo.1) | copy-start | bytes 393220
  1.6 3.2 %copy-start.3 = (bf16[3,128,128]{2,1,0:T(8,128)(2,1)S(1)}, bf16[3,128,128]{2,1,0:T(8,128)(2,1)}, u32[]{:S(2)}) copy-start(bf16[3,128,128]{2,1,0:T(8,128)(2,1)} %ckvo.1) | copy-start | bytes 294916
  1.6 3.2 %copy-start.4 = (bf16[3,128,128]{2,1,0:T(8,128)(2,1)S(1)}, bf16[3,128,128]{2,1,0:T(8,128)(2,1)}, u32[]{:S(2)}) copy-start(bf16[3,128,128]{2,1,0:T(8,128)(2,1)} %rkvo.1) | copy-start | bytes 294916
  1.6 3.2 %copy-start.5 = (bf16[128,128]{1,0:T(8,128)(2,1)S(1)}, bf16[128,128]{1,0:T(8,128)(2,1)}, u32[]{:S(2)}) copy-start(bf16[128,128]{1,0:T(8,128)(2,1)} %iq_w.1) | copy-start | bytes 98308
  1.6 3.2 %copy-start.6 = (bf16[128,128]{1,0:T(8,128)(2,1)S(1)}, bf16[128,128]{1,0:T(8,128)(2,1)}, u32[]{:S(2)}) copy-start(bf16[128,128]{1,0:T(8,128)(2,1)} %cq_w.1) | copy-start | bytes 98308
  1.6 3.2 %copy-start.7 = (bf16[96,128]{1,0:T(8,128)(2,1)S(1)}, bf16[96,128]{1,0:T(8,128)(2,1)}, u32[]{:S(2)}) copy-start(bf16[96,128]{1,0:T(8,128)(2,1)} %ind.1) | copy-start | bytes 73732
  1.6 3.2 %copy-start.8 = (bf16[10,512]{1,0:T(8,128)(2,1)S(1)}, bf16[10,512]{1,0:T(8,128)(2,1)}, u32[]{:S(2)}) copy-start(bf16[10,512]{1,0:T(8,128)(2,1)} %table.1) | copy-start | bytes 30724
  1.6 3.2 %copy-start.9 = (bf16[4,128]{1,0:T(4,128)(2,1)S(1)}, bf16[4,128]{1,0:T(4,128)(2,1)}, u32[]{:S(2)}) copy-start(bf16[4,128]{1,0:T(4,128)(2,1)} %ct.1) | copy-start | bytes 3076

commit v2 on v1

--- a/solution.py
+++ b/solution.py
@@ -113,14 +113,22 @@
 
 def finish(acc, den, out_ref):
     n_class, width, n_rows = acc.shape
-    n_parts, out_rows, _ = out_ref.shape
-    for c in range(n_class):
-        numer = acc[c].T.astype(BF16).reshape(n_parts, out_rows, width)
-        out_ref[:, :, c * width : (c + 1) * width] = numer
+    _, _, n_outer, out_rows, _ = out_ref.shape
     d = den[...]
     pad = jnp.zeros((width - d.shape[0], n_rows), F32)
-    d = jnp.concatenate([d, pad], axis=0).T.astype(BF16)
-    out_ref[:, :, n_class * width :] = d.reshape(n_parts, out_rows, width)
+    pieces = [acc[c] for c in range(n_class)] + [jnp.concatenate([d, pad], axis=0)]
+    for i, piece in enumerate(pieces):
+        rows = piece.T.astype(BF16).reshape(n_outer, 2, 2, out_rows, width)
+        for b in range(2):
+            for c in range(2):
+                out_ref[c, b, :, :, i * width : (i + 1) * width] = rows[:, b, c]
+
+
+def column(row, first, n):
+    shape = (n, row.shape[1])
+    wanted = lax.broadcasted_iota(jnp.int32, shape, 0) + first
+    here = lax.broadcasted_iota(jnp.int32, shape, 1) == wanted
+    return jnp.sum(jnp.where(here, jnp.broadcast_to(row, shape), 0.0), axis=1, keepdims=True)
 
 
 def embed_rows(total, ct, cq_w, rkvo, context, labels, table):
@@ -185,23 +193,31 @@
 
 
 def window_kernel(
-    n_src, n_split, src, mask_src, context, labels, ind, iq_w, ckvo, cqkvo, ct, cq_w, rkvo, table, icl_q, icl_kvo,
-    out_ref, xbuf, mbuf, sums, pbuf, own_in, gbuf, wcol, wrow, wt, acc, den,
-    x_send, x_recv, x_local, m_send, m_recv, p_send, p_recv, g_send, g_recv, local,
+    n_src, n_split, src, context, labels, ind, iq_w, ckvo, cqkvo, ct, cq_w, rkvo, table, icl_q, icl_kvo,
+    out_ref, xbuf, mask_src, mbuf, sums, core_in, core_sum, near_in, near_sum, pbuf, gbuf, wcol, wrow, wt, acc, den,
+    x_send, x_recv, x_local, m_send, m_recv, pair_send, pair_recv, p_send, p_recv, g_send, g_recv, far_recv, local,
 ):
     n_chunk, _, per, n_rows, width = xbuf.shape
     n_class = ct.shape[0]
-    n_parts, out_rows, _ = pbuf.shape
+    n_outer, out_rows, _ = pbuf.shape
+    n_parts = n_outer * 4
     all_rows = n_src * n_rows
     me = lax.axis_index("row")
     part = me * n_split + lax.axis_index("feat")
 
+    outer, inner = part // 4, lax.rem(part, 4)
+    flags = jnp.where(context[...] == 1, 1.0, 0.0)
+    mask_src[...] = jnp.broadcast_to(column(flags, 0, n_rows), mask_src.shape).astype(BF16)
+
+    def device(p):
+        return {"row": p // n_split, "feat": lax.rem(p, n_split)}
+
     barrier = pltpu.get_barrier_semaphore()
 
     def greet(d, carry):
         peer = lax.rem(part + d, n_parts)
         pl.semaphore_signal(
-            barrier, inc=1, device_id={"row": peer // n_split, "feat": lax.rem(peer, n_split)}, device_id_type=MESH
+            barrier, inc=1, device_id=device(peer), device_id_type=MESH
         )
         return carry
 
@@ -255,38 +271,67 @@
     lax.fori_loop(0, n_chunk, work, 0)
     finish(acc, den, sums)
 
-    def exchange(make):
-        def send(d, carry):
-            peer = lax.rem(part + d, n_parts)
-            make(peer, {"row": peer // n_split, "feat": lax.rem(peer, n_split)}).start()
-            return carry
-
-        lax.fori_loop(1, n_parts, send, 0)
-
-    exchange(
-        lambda peer, device: pltpu.make_async_remote_copy(
-            src_ref=sums.at[peer], dst_ref=pbuf.at[part], send_sem=p_send, recv_sem=p_recv,
-            device_id=device, device_id_type=MESH,
-        )
+    own_core, own_near = lax.rem(inner, 2), inner // 2
+    pair = pltpu.make_async_remote_copy(
+        src_ref=sums.at[1 - own_core], dst_ref=core_in, send_sem=pair_send.at[0], recv_sem=pair_recv.at[0],
+        device_id=device(part + 1 - 2 * own_core), device_id_type=MESH,
     )
-    own_sums = pltpu.make_async_copy(sums.at[part], pbuf.at[part], local.at[1])
-    own_sums.start()
+    pair.start()
     mask = jnp.transpose(mbuf[...].reshape(all_rows, width).astype(F32))[:1]
-    own_sums.wait()
-    wait_bytes(pbuf.at[pl.ds(0, n_parts - 1)], p_recv)
+    pair.wait()
+    core_sum[...] = (sums[own_core].astype(F32) + core_in[...].astype(F32)).astype(BF16)
+    pair = pltpu.make_async_remote_copy(
+        src_ref=core_sum.at[1 - own_near], dst_ref=near_in, send_sem=pair_send.at[1], recv_sem=pair_recv.at[1],
+        device_id=device(part + 2 - 4 * own_near), device_id_type=MESH,
+    )
+    pair.start()
+    pair.wait()
+    near_sum[...] = (core_sum[own_near].astype(F32) + near_in[...].astype(F32)).astype(BF16)
+
+    def send_sums(d, carry):
+        peer = lax.rem(outer + d, n_outer)
+        pltpu.make_async_remote_copy(
+            src_ref=near_sum.at[peer], dst_ref=pbuf.at[outer], send_sem=p_send, recv_sem=p_recv,
+            device_id=device(peer * 4 + inner), device_id_type=MESH,
+        ).start()
+        return carry
+
+    lax.fori_loop(1, n_outer, send_sums, 0)
+    pbuf[outer] = near_sum[outer]
+    wait_bytes(pbuf.at[pl.ds(0, n_outer - 1)], p_recv)
     total = jnp.sum(pbuf[...].astype(F32), axis=0)
-    embed, inputs = embed_rows(total, ct, cq_w, rkvo, context[...], labels[...], table)
-    own_in[...] = inputs
-    exchange(
-        lambda peer, device: pltpu.make_async_remote_copy(
-            src_ref=own_in, dst_ref=gbuf.at[part], send_sem=g_send, recv_sem=g_recv,
-            device_id=device, device_id_type=MESH,
-        )
-    )
-    own_inputs = pltpu.make_async_copy(own_in, gbuf.at[part], local.at[2])
-    own_inputs.start()
-    own_inputs.wait()
-    wait_bytes(gbuf.at[pl.ds(0, n_parts - 1)], g_recv)
+    own_flags = column(flags, lax.axis_index("feat") * out_rows, out_rows)
+    own_labels = column(labels[...].astype(F32), 0, out_rows).astype(jnp.int32)
+    embed, inputs = embed_rows(total, ct, cq_w, rkvo, own_flags, own_labels, table)
+    gbuf[part] = inputs
+
+    def send_far(d, carry):
+        peer = lax.rem(outer + d, n_outer)
+        pltpu.make_async_remote_copy(
+            src_ref=gbuf.at[part], dst_ref=gbuf.at[part], send_sem=g_send, recv_sem=far_recv.at[outer],
+            device_id=device(peer * 4 + inner), device_id_type=MESH,
+        ).start()
+        return carry
+
+    lax.fori_loop(1, n_outer, send_far, 0)
+
+    def send_near(slot):
+        for d in range(1, 4):
+            pltpu.make_async_remote_copy(
+                src_ref=gbuf.at[slot], dst_ref=gbuf.at[slot], send_sem=g_send, recv_sem=g_recv,
+                device_id=device(outer * 4 + lax.rem(inner + d, 4)), device_id_type=MESH,
+            ).start()
+
+    send_near(part)
+
+    def forward(d, carry):
+        peer = lax.rem(outer + d, n_outer)
+        wait_bytes(gbuf.at[peer * 4 + inner], far_recv.at[peer])
+        send_near(peer * 4 + inner)
+        return carry
+
+    lax.fori_loop(1, n_outer, forward, 0)
+    wait_bytes(gbuf.at[pl.ds(0, 3 * n_outer)], g_recv)
     window = gbuf[...].reshape(all_rows, n_class * width)
     out_ref[...] = in_context(embed, window, mask, icl_q, icl_kvo)
 
@@ -297,7 +342,7 @@
         return carry
 
     lax.fori_loop(0, n_chunk, sent, 0)
-    wait_bytes(pbuf.at[pl.ds(0, n_parts - 1)], p_send)
+    wait_bytes(pbuf.at[pl.ds(0, n_outer - 1)], p_send)
     wait_bytes(gbuf.at[pl.ds(0, n_parts - 1)], g_send)
 
 
@@ -328,23 +373,25 @@
     per_chunk = 2 if own_feat % 2 == 0 else 1
     n_chunk = own_feat // per_chunk
     d3 = n_class * width
-    flags = (is_context == 1).astype(F32)
-    mask = jnp.broadcast_to(flags.astype(BF16)[:, None], (n_rows, width))
+    n_outer = n_parts // 4
     by_feature = jnp.transpose(cells, (1, 0, 2)).reshape(n_src, n_chunk, per_chunk, n_rows, width)
-    own = lax.dynamic_slice_in_dim(flags, lax.axis_index("feat") * out_rows, out_rows)
     vmem = pl.BlockSpec(memory_space=pltpu.VMEM)
     dma = pltpu.SemaphoreType.DMA
     return pl.pallas_call(
         functools.partial(window_kernel, n_src, n_split),
-        in_specs=[pl.BlockSpec(memory_space=pl.ANY)] + [vmem] * 13,
+        in_specs=[pl.BlockSpec(memory_space=pl.ANY)] + [vmem] * 12,
         out_specs=vmem,
         out_shape=jax.ShapeDtypeStruct((out_rows, d3), BF16),
         scratch_shapes=[
             pltpu.VMEM((n_chunk, n_src, per_chunk, n_rows, width), BF16),
+            pltpu.VMEM((n_rows, width), BF16),
             pltpu.VMEM((n_src, n_rows, width), BF16),
-            pltpu.VMEM((n_parts, out_rows, d3 + width), BF16),
-            pltpu.VMEM((n_parts, out_rows, d3 + width), BF16),
-            pltpu.VMEM((out_rows, d3), BF16),
+            pltpu.VMEM((2, 2, n_outer, out_rows, d3 + width), BF16),
+            pltpu.VMEM((2, n_outer, out_rows, d3 + width), BF16),
+            pltpu.VMEM((2, n_outer, out_rows, d3 + width), BF16),
+            pltpu.VMEM((n_outer, out_rows, d3 + width), BF16),
+            pltpu.VMEM((n_outer, out_rows, d3 + width), BF16),
+            pltpu.VMEM((n_outer, out_rows, d3 + width), BF16),
             pltpu.VMEM((n_parts, out_rows, d3), BF16),
             pltpu.VMEM((HEADS * n_ind, width), BF16),
             pltpu.VMEM((n_class * ROW_HEADS, width), BF16),
@@ -356,20 +403,22 @@
             dma((n_chunk,)),
             dma,
             dma,
-            dma,
-            dma,
-            dma,
-            dma,
-            dma((3,)),
+            dma((2,)),
+            dma((2,)),
+            dma,
+            dma,
+            dma,
+            dma,
+            dma((n_outer,)),
+            dma((1,)),
         ],
         compiler_params=pltpu.CompilerParams(
             vmem_limit_bytes=48 * 2**20, collective_id=0, has_side_effects=True
         ),
     )(
         by_feature,
-        mask,
-        own[:, None],
-        labels[:, None],
+        is_context[None, :],
+        labels[None, :],
         inducing,
         induce_query,
         column_kvo,

time: 94.6 us -> 87.2 us (0.922)
  the two profiles are of different devices: /device:TPU:29 before, /device:TPU:0 now
where the time goes in v2:
time: 87.2 us; the launch traced here: 86.7 us
  Pallas kernels  82.8 us (95%)
  local copies, waits for them, and re-layouts  3.76 us (4%)
    pallas_call x1, Pallas kernels, on_device(): pl.pallas_call(functools.partial(window_kernel, n_src, n_split), in_specs...  82.8 us
    transpose x1, local copies, waits for them, and re-layouts, on_device(): jnp.transpose(cells, (1, 0, 2))  3.09 us

profile of v2, /device:TPU:0, one launch (start us, length us, event | category | flops | bytes accessed | tf_op | source)
XLA Modules:
  0.0 86.7 jit_solution(249335926859308564)
XLA Ops:
  0.0 0.0 copy-start
  0.0 0.0 copy-start.1
  0.0 0.0 copy-start.2
  0.0 0.0 copy-start.3
  0.0 0.0 copy-start.4
  0.0 0.0 copy-start.5
  0.0 0.0 copy-start.6
  0.0 0.0 copy-start.7
  0.0 0.0 copy-start.8
  0.1 0.0 copy-start.9
  0.1 0.0 copy-start.10
  0.1 0.0 copy-start.11
  0.1 3.1 %copy.14 = bf16[256,32,128]{2,1,0:T(8,128)(2,1)S(1)} copy(bf16[256,32,128]{2,0,1:T(8,128)(2,1)} %bitcast.7) | data formatting | bytes 4194304 | tf_op jit(solution)/shard_map/transpose | solution.py:377
  3.2 0.0 copy-done
  3.2 0.0 copy-done.1
  3.2 0.0 copy-done.2
  3.2 0.0 copy-done.3
  3.2 0.0 copy-done.4
  3.2 0.0 copy-done.5
  3.2 0.0 copy-done.6
  3.3 0.0 copy-done.7
  3.3 0.0 copy-done.8
  3.3 0.0 copy-done.9
  3.3 0.0 copy-done.10
  3.3 0.0 copy-done.11
  3.3 82.8 %shard_map.127 = bf16[32,512]{1,0:T(8,128)(2,1)S(1)} custom-call(bf16[16,8,2,32,128]{4,3,2,1,0:T(8,128)(2,1)S(1)} %bitcast.4, s32[1,32]{1,0:T(1,128)S(1)} %bitcast.5, s32[1,32]{1,0:T(1,128)S(1)} %bitcast.6, bf16[96,128]{1,0:T(8,128)(2,1)S(1)} %copy-done.7, bf16[128,128]{1,0:T(8,128)(2,1)S(1)} %copy-done.5, bf16[3,128,128]{2,1,0:T(8,128)(2,1)S(1)} %copy-done.3, ...), custom_call_target="tpu_custom_call" | custom-call | tf_op jit(solution)/shard_map/pallas_call | solution.py:380
  86.1 0.6 copy.16
Async XLA Ops:
  0.0 3.2 %copy-start = (bf16[3,512,512]{2,1,0:T(8,128)(2,1)S(1)}, bf16[3,512,512]{2,1,0:T(8,128)(2,1)}, u32[]{:S(2)}) copy-start(bf16[3,512,512]{2,1,0:T(8,128)(2,1)} %icl_kvo.1) | copy-start | bytes 4718596
  0.0 3.2 %copy-start.1 = (bf16[512,512]{1,0:T(8,128)(2,1)S(1)}, bf16[512,512]{1,0:T(8,128)(2,1)}, u32[]{:S(2)}) copy-start(bf16[512,512]{1,0:T(8,128)(2,1)} %icl_q.1) | copy-start | bytes 1572868
  0.0 3.2 %copy-start.2 = (bf16[4,128,128]{2,1,0:T(8,128)(2,1)S(1)}, bf16[4,128,128]{2,1,0:T(8,128)(2,1)}, u32[]{:S(2)}) copy-start(bf16[4,128,128]{2,1,0:T(8,128)(2,1)} %cqkvo.1) | copy-start | bytes 393220
  0.0 3.2 %copy-start.3 = (bf16[3,128,128]{2,1,0:T(8,128)(2,1)S(1)}, bf16[3,128,128]{2,1,0:T(8,128)(2,1)}, u32[]{:S(2)}) copy-start(bf16[3,128,128]{2,1,0:T(8,128)(2,1)} %ckvo.1) | copy-start | bytes 294916
  0.0 3.2 %copy-start.4 = (bf16[3,128,128]{2,1,0:T(8,128)(2,1)S(1)}, bf16[3,128,128]{2,1,0:T(8,128)(2,1)}, u32[]{:S(2)}) copy-start(bf16[3,128,128]{2,1,0:T(8,128)(2,1)} %rkvo.1) | copy-start | bytes 294916
  0.0 3.2 %copy-start.5 = (bf16[128,128]{1,0:T(8,128)(2,1)S(1)}, bf16[128,128]{1,0:T(8,128)(2,1)}, u32[]{:S(2)}) copy-start(bf16[128,128]{1,0:T(8,128)(2,1)} %iq_w.1) | copy-start | bytes 98308
  0.0 3.2 %copy-start.6 = (bf16[128,128]{1,0:T(8,128)(2,1)S(1)}, bf16[128,128]{1,0:T(8,128)(2,1)}, u32[]{:S(2)}) copy-start(bf16[128,128]{1,0:T(8,128)(2,1)} %cq_w.1) | copy-start | bytes 98308
  0.0 3.2 %copy-start.7 = (bf16[96,128]{1,0:T(8,128)(2,1)S(1)}, bf16[96,128]{1,0:T(8,128)(2,1)}, u32[]{:S(2)}) copy-start(bf16[96,128]{1,0:T(8,128)(2,1)} %ind.1) | copy-start | bytes 73732
  0.0 3.2 %copy-start.8 = (bf16[10,512]{1,0:T(8,128)(2,1)S(1)}, bf16[10,512]{1,0:T(8,128)(2,1)}, u32[]{:S(2)}) copy-start(bf16[10,512]{1,0:T(8,128)(2,1)} %table.1) | copy-start | bytes 30724
  0.1 3.2 %copy-start.9 = (bf16[4,128]{1,0:T(4,128)(2,1)S(1)}, bf16[4,128]{1,0:T(4,128)(2,1)}, u32[]{:S(2)}) copy-start(bf16[4,128]{1,0:T(4,128)(2,1)} %ct.1) | copy-start | bytes 3076
  0.1 3.2 %copy-start.10 = (s32[32]{0:T(128)S(1)}, s32[32]{0:T(128)}, u32[]{:S(2)}) copy-start(s32[32]{0:T(128)} %param.14) | copy-start | bytes 388
  0.1 3.2 %copy-start.11 = (s32[32]{0:T(128)S(1)}, s32[32]{0:T(128)}, u32[]{:S(2)}) copy-start(s32[32]{0:T(128)} %param.15) | copy-start | bytes 388
